TPU v7x, 32 devices: a whole 2x2x4 slice. The times are simulated.
32 devices in a mesh: dp: 4 (over y, core), wide: 4 (over z), narrow: 2 (over x).
Axes of the slice: x: 2, y: 2, z: 4, core: 2. Of those that a mesh axis runs over, the one named last changes fastest.
Arguments:
- streams: bfloat16 [4, 1024, 2048], P(None, 'dp', ('wide', 'narrow')), may hold values from -6 to 6
- prior: bfloat16 [12, 1024, 2048], P(None, 'dp', ('wide', 'narrow')), may hold values from -6 to 6
- streams_grad: bfloat16 [4, 1024, 2048], P(None, 'dp', ('wide', 'narrow')), may hold values from -6 to 6
- w_qkv: bfloat16 [3, 2048, 2048], P(None, 'wide', 'narrow')
- qkv_bias: bfloat16 [3, 2048], P(None, ('narrow', 'wide')), may hold values from -3 to 3
- w_out: bfloat16 [2048, 2048], P('narrow', 'wide'), may hold values from -1.5 to 1.5
- w_up: bfloat16 [2048, 8192], P('wide', 'narrow')
- up_bias: bfloat16 [8192], P(('narrow', 'wide')), may hold values from -3 to 3
- w_down: bfloat16 [8192, 2048], P('narrow', 'wide'), may hold values from -0.0625 to 0.0625
- branch_bias: bfloat16 [2048], P(('wide', 'narrow')), may hold values from -3 to 3
- norm_gain: bfloat16 [4, 2048], P(None, ('wide', 'narrow')), may hold values from 0.25 to 1.75
- norm_bias: bfloat16 [4, 2048], P(None, ('wide', 'narrow')), may hold values from -2 to 2
- mix_gain: bfloat16 [2048], P(('wide', 'narrow')), may hold values from 0.099609375 to 1.8984375
- mix_in: bfloat16 [2048, 52], P(('wide', 'narrow')), may hold values from -0.125 to 0.125
- mix_out: bfloat16 [52, 52], replicated, may hold values from -0.875 to 0.875
- mix_static: bfloat16 [52], replicated, may hold values from -3 to 3
Outputs:
- streams_out: bfloat16 [4, 1024, 2048], P(None, 'dp', ('wide', 'narrow'))
- streams_in_grad: bfloat16 [4, 1024, 2048], P(None, 'dp', ('wide', 'narrow'))
- prior_grad: bfloat16 [12, 1024, 2048], P(None, 'dp', ('wide', 'narrow'))
- w_qkv_grad: float32 [3, 2048, 2048], P(None, 'wide', 'narrow')
- qkv_bias_grad: float32 [3, 2048], P(None, ('narrow', 'wide'))
- w_out_grad: float32 [2048, 2048], P('narrow', 'wide')
- w_up_grad: float32 [2048, 8192], P('wide', 'narrow')
- up_bias_grad: float32 [8192], P(('narrow', 'wide'))
- w_down_grad: float32 [8192, 2048], P('narrow', 'wide')
- branch_bias_grad: float32 [2048], P(('wide', 'narrow'))
- norm_gain_grad: float32 [4, 2048], P(None, ('wide', 'narrow'))
- norm_bias_grad: float32 [4, 2048], P(None, ('wide', 'narrow'))
- mix_gain_grad: float32 [2048], P(('wide', 'narrow'))
- mix_in_grad: float32 [2048, 52], P(('wide', 'narrow'))
- mix_out_grad: float32 [52, 52], replicated
- mix_static_grad: float32 [52], replicated
All inputs are finite; a program needn't handle non-finite values.
Results may differ from a plain program's by a relative error of at most 0.02.
Values may be sent and summed in bfloat16 or wider, within the bound.
No kernel may reach another device: no remote copies, remote signals or barrier semaphores. Data moves between devices by JAX's collectives and lax.ppermute only.
A program may use at most 192 MiB of HBM per device.

v0:
```python
import math
import jax
import jax.numpy as jnp
from jax import lax
from jax.sharding import PartitionSpec as P

D = 2048
HD = 128
ROT = 32
MIXH = 52
STACK = 13
norm_eps = 1e-05
rms_eps = 1e-06


def model_sum(parts):
    return lax.psum(parts, ("wide", "narrow"))


def gelu_exact(inputs):
    return 0.5 * inputs * (1.0 + lax.erf(inputs * (1.0 / math.sqrt(2.0))))


def gelu_slope(inputs):
    normal_cdf = 0.5 * (1.0 + lax.erf(inputs * (1.0 / math.sqrt(2.0))))
    return normal_cdf + inputs * jnp.exp(-0.5 * inputs * inputs) * (1.0 / math.sqrt(2.0 * math.pi))


def rotate(heads_in, cosine, sine_table, direction):
    half = ROT // 2
    first = heads_in[..., :half]
    second = heads_in[..., half:ROT]
    rest_part = heads_in[..., ROT:]
    cos_b = cosine[:, None, :]
    sin_b = direction * sine_table[:, None, :]
    return jnp.concatenate(
        [first * cos_b - second * sin_b, second * cos_b + first * sin_b, rest_part], axis=-1
    )


def masked_scores(query_rows, key_heads, row_start, row_block, length, scale):
    scores = (
        jnp.einsum("qhd,khd->hqk", query_rows, key_heads, preferred_element_type=jnp.float32)
        * scale
    )
    row_ids = row_start + lax.broadcasted_iota(jnp.int32, (row_block, length), 0)
    col_ids = lax.broadcasted_iota(jnp.int32, (row_block, length), 1)
    return jnp.where((col_ids <= row_ids)[None], scores, -1e30)


def attend_rows(queries, key_heads, value_heads, scale):
    length = queries.shape[0]
    row_block = min(512, length)

    def one_block(block_index):
        row_start = block_index * row_block
        scores = masked_scores(queries, key_heads, row_start, row_block, length, scale)
        row_top = jnp.max(scores, axis=2, keepdims=True)
        log_total = row_top + jnp.log(jnp.sum(jnp.exp(scores - row_top), axis=2, keepdims=True))
        attn_probs = jnp.exp(scores - log_total).astype(jnp.bfloat16)
        output = jnp.einsum(
            "hqk,khd->qhd", attn_probs, value_heads, preferred_element_type=jnp.float32
        )
        return (output, log_total[:, :, 0])

    outputs, totals = lax.map(one_block, jnp.arange(length // row_block, dtype=jnp.int32))
    return (outputs.reshape(queries.shape), totals)


def attend_back(queries, key_heads, value_heads, out_grad, totals, scale):
    length = queries.shape[0]
    row_block = min(512, length)

    def one_block(carry, block_index):
        key_grad, value_grad = carry
        row_start = block_index * row_block
        log_total = lax.dynamic_index_in_dim(totals, block_index, 0, keepdims=False)
        scores = masked_scores(queries, key_heads, row_start, row_block, length, scale)
        attn_probs = jnp.exp(scores - log_total[:, :, None])
        probs_low = attn_probs.astype(jnp.bfloat16)
        value_grad = value_grad + jnp.einsum(
            "hqk,qhd->khd", probs_low, out_grad, preferred_element_type=jnp.float32
        )
        prob_grad = jnp.einsum(
            "qhd,khd->hqk", out_grad, value_heads, preferred_element_type=jnp.float32
        )
        row_dot = jnp.sum(attn_probs * prob_grad, axis=2, keepdims=True)
        score_grad = (attn_probs * (prob_grad - row_dot)).astype(jnp.bfloat16)
        query_grad = (
            jnp.einsum("hqk,khd->qhd", score_grad, key_heads, preferred_element_type=jnp.float32)
            * scale
        )
        key_grad = (
            key_grad
            + jnp.einsum("hqk,qhd->khd", score_grad, queries, preferred_element_type=jnp.float32)
            * scale
        )
        return ((key_grad, value_grad), query_grad)

    zero_heads = jnp.zeros(queries.shape, jnp.float32)
    (key_grad, value_grad), query_blocks = lax.scan(
        one_block, (zero_heads, zero_heads), jnp.arange(length // row_block, dtype=jnp.int32)
    )
    return (query_blocks.reshape(queries.shape), key_grad, value_grad)


def contract_rows(left, right):
    return lax.dot_general(
        left, right, (((0,), (0,)), ((), ())), preferred_element_type=jnp.float32
    )


def contract_cols(left, right):
    return lax.dot_general(
        left, right, (((1,), (1,)), ((), ())), preferred_element_type=jnp.float32
    )


def per_device(
    streams,
    prior,
    streams_grad,
    w_qkv,
    qkv_bias,
    w_out,
    w_up,
    up_bias,
    w_down,
    branch_bias,
    norm_gain,
    norm_bias,
    mix_gain,
    mix_in,
    mix_out,
    mix_static,
):
    high = lax.Precision.HIGHEST
    length = streams.shape[1]
    local_cols = streams.shape[2]
    heads_here = local_cols // HD
    scale = 1.0 / math.sqrt(HD)
    inputs = streams.astype(jnp.float32)
    row_total, row_squares = model_sum((jnp.sum(inputs, axis=2), jnp.sum(inputs * inputs, axis=2)))
    row_mean = row_total / D
    inv_std = lax.rsqrt(row_squares / D - row_mean * row_mean + norm_eps)
    centred = (inputs - row_mean[:, :, None]) * inv_std[:, :, None]
    norm_scale = norm_gain.astype(jnp.float32)[:, None, :]
    normed = (centred * norm_scale + norm_bias.astype(jnp.float32)[:, None, :]).astype(jnp.bfloat16)
    near_cols = lax.all_gather(normed, "narrow", axis=2, tiled=True)
    qkv_part = jnp.einsum("std,sdf->stf", near_cols[:3], w_qkv, preferred_element_type=jnp.float32)
    up_part = jnp.dot(near_cols[3], w_up, preferred_element_type=jnp.float32)
    qkv_pre, up_summed = (
        lax.psum_scatter(qkv_part, "wide", scatter_dimension=2, tiled=True),
        lax.psum_scatter(up_part[None], "wide", scatter_dimension=2, tiled=True),
    )
    up_pre = up_summed[0]
    qkv_pre = qkv_pre + qkv_bias.astype(jnp.float32)[:, None, :]
    up_pre = up_pre + up_bias.astype(jnp.float32)[None, :]
    positions = lax.iota(jnp.float32, length)
    freqs = jnp.exp(lax.iota(jnp.float32, ROT // 2) * (-2.0 * math.log(10000.0) / ROT))
    angles = positions[:, None] * freqs[None, :]
    cosine = jnp.cos(angles)
    sine_table = jnp.sin(angles)
    head_view = qkv_pre.reshape(3, length, heads_here, HD)
    queries = rotate(head_view[0], cosine, sine_table, 1.0).astype(jnp.bfloat16)
    key_heads = rotate(head_view[1], cosine, sine_table, 1.0).astype(jnp.bfloat16)
    value_heads = head_view[2].astype(jnp.bfloat16)
    attn_heads, totals = attend_rows(queries, key_heads, value_heads, scale)
    attn_low = attn_heads.reshape(length, local_cols).astype(jnp.bfloat16)
    hidden = gelu_exact(up_pre).astype(jnp.bfloat16)
    attn_wide, hidden_wide = (
        lax.all_gather(attn_low, "wide", axis=1, tiled=True),
        lax.all_gather(hidden, "wide", axis=1, tiled=True),
    )
    branch_part = jnp.dot(attn_wide, w_out, preferred_element_type=jnp.float32) + jnp.dot(
        hidden_wide, w_down, preferred_element_type=jnp.float32
    )
    branch = (
        lax.psum_scatter(branch_part, "narrow", scatter_dimension=1, tiled=True)
        + branch_bias.astype(jnp.float32)[None, :]
    )
    layer_out = inputs[3] + branch
    mix_scale = mix_gain.astype(jnp.float32)
    scaled = layer_out * mix_scale[None, :]
    mix_weight = mix_in.astype(jnp.float32)
    mix_back = mix_out.astype(jnp.float32)
    energy, logit_sum = model_sum(
        (jnp.sum(layer_out * layer_out, axis=1), jnp.dot(scaled, mix_weight, precision=high))
    )
    rms = lax.rsqrt(energy / D + rms_eps)
    logits = logit_sum * rms[:, None]
    mix_hidden = gelu_exact(logits)
    weights = (
        jnp.dot(mix_hidden, mix_back, precision=high) + mix_static.astype(jnp.float32)[None, :]
    )
    coef = weights.reshape(length, 4, STACK)
    prior_vals = prior.astype(jnp.float32)
    mixed = jnp.einsum("tsj,jtl->stl", coef[:, :, : STACK - 1], prior_vals, precision=high)
    streams_out = (
        mixed + jnp.transpose(coef[:, :, STACK - 1])[:, :, None] * layer_out[None]
    ).astype(jnp.bfloat16)
    grad_out = streams_grad.astype(jnp.float32)
    prior_part = jnp.einsum("stl,jtl->tsj", grad_out, prior_vals, precision=high)
    layer_part = jnp.einsum("stl,tl->ts", grad_out, layer_out, precision=high)
    coef_part = jnp.concatenate([prior_part, layer_part[:, :, None]], axis=2).reshape(length, MIXH)
    (coef_grad,) = model_sum((coef_part,))
    prior_grad = jnp.einsum(
        "tsj,stl->jtl", coef[:, :, : STACK - 1], grad_out, precision=high
    ).astype(jnp.bfloat16)
    layer_grad = jnp.einsum("ts,stl->tl", coef[:, :, STACK - 1], grad_out, precision=high)
    static_grad = jnp.sum(coef_grad, axis=0)
    mix_out_grad = jnp.dot(mix_hidden.T, coef_grad, precision=high)
    logit_grad = jnp.dot(coef_grad, mix_back.T, precision=high) * gelu_slope(logits)
    sum_grad = logit_grad * rms[:, None]
    rms_grad = jnp.sum(logit_grad * logit_sum, axis=1)
    energy_grad = -0.5 * rms_grad * rms * rms * rms / D
    mix_in_grad = jnp.dot(scaled.T, sum_grad, precision=high)
    scaled_grad = jnp.dot(sum_grad, mix_weight.T, precision=high)
    mix_gain_grad = jnp.sum(scaled_grad * layer_out, axis=0)
    layer_grad = (
        layer_grad + scaled_grad * mix_scale[None, :] + 2.0 * energy_grad[:, None] * layer_out
    )
    branch_grad = layer_grad.astype(jnp.bfloat16)
    branch_bias_grad = jnp.sum(branch_grad.astype(jnp.float32), axis=0)
    branch_near = lax.all_gather(branch_grad, "narrow", axis=1, tiled=True)
    attn_grad, hidden_grad = (
        lax.psum_scatter(
            contract_cols(branch_near, w_out), "wide", scatter_dimension=1, tiled=True
        ),
        lax.psum_scatter(
            contract_cols(branch_near, w_down), "wide", scatter_dimension=1, tiled=True
        ),
    )
    out_weight_grad = contract_rows(attn_wide, branch_near)
    down_weight_grad = contract_rows(hidden_wide, branch_near)
    attn_low_grad = attn_grad.astype(jnp.bfloat16).reshape(length, heads_here, HD)
    up_grad = (hidden_grad * gelu_slope(up_pre)).astype(jnp.bfloat16)
    up_bias_grad = jnp.sum(up_grad.astype(jnp.float32), axis=0)
    query_grad, key_grad, value_grad = attend_back(
        queries, key_heads, value_heads, attn_low_grad, totals, scale
    )
    query_pre = rotate(query_grad, cosine, sine_table, -1.0).reshape(length, local_cols)
    key_pre = rotate(key_grad, cosine, sine_table, -1.0).reshape(length, local_cols)
    projected_grad = jnp.stack([query_pre, key_pre, value_grad.reshape(length, local_cols)]).astype(
        jnp.bfloat16
    )
    qkv_bias_grad = jnp.sum(projected_grad.astype(jnp.float32), axis=1)
    far_qkv, far_up = (
        lax.all_gather(projected_grad, "wide", axis=2, tiled=True),
        lax.all_gather(up_grad[None], "wide", axis=2, tiled=True),
    )
    qkv_weight_grad = jnp.einsum(
        "std,stf->sdf", near_cols[:3], far_qkv, preferred_element_type=jnp.float32
    )
    up_weight_grad = contract_rows(near_cols[3], far_up[0])
    normed_part = jnp.concatenate(
        [
            jnp.einsum("stf,sdf->std", far_qkv, w_qkv, preferred_element_type=jnp.float32),
            contract_cols(far_up[0], w_up)[None],
        ],
        axis=0,
    )
    normed_grad = lax.psum_scatter(normed_part, "narrow", scatter_dimension=2, tiled=True)
    gain_grad = jnp.sum(normed_grad * centred, axis=1)
    shift_grad = jnp.sum(normed_grad, axis=1)
    centred_grad = normed_grad * norm_scale
    grad_total, grad_cross = model_sum(
        (jnp.sum(centred_grad, axis=2), jnp.sum(centred_grad * centred, axis=2))
    )
    input_grad = inv_std[:, :, None] * (
        centred_grad - (grad_total / D)[:, :, None] - centred * (grad_cross / D)[:, :, None]
    )
    input_grad = input_grad.at[3].add(layer_grad)
    streams_in_grad = input_grad.astype(jnp.bfloat16)
    summed = lax.psum(
        (
            qkv_weight_grad,
            qkv_bias_grad,
            out_weight_grad,
            up_weight_grad,
            up_bias_grad,
            down_weight_grad,
            branch_bias_grad,
            gain_grad,
            shift_grad,
            mix_gain_grad,
            mix_in_grad,
            mix_out_grad,
            static_grad,
        ),
        "dp",
    )
    return (
        streams_out,
        streams_in_grad,
        prior_grad,
        summed[0],
        summed[1],
        summed[2],
        summed[3],
        summed[4],
        summed[5],
        summed[6],
        summed[7],
        summed[8],
        summed[9],
        summed[10],
        summed[11],
        summed[12],
    )


def solution(mesh):
    return jax.shard_map(
        per_device,
        mesh=mesh,
        in_specs=(
            P(None, "dp", ("wide", "narrow")),
            P(None, "dp", ("wide", "narrow")),
            P(None, "dp", ("wide", "narrow")),
            P(None, "wide", "narrow"),
            P(None, ("narrow", "wide")),
            P("narrow", "wide"),
            P("wide", "narrow"),
            P(("narrow", "wide")),
            P("narrow", "wide"),
            P(("wide", "narrow")),
            P(None, ("wide", "narrow")),
            P(None, ("wide", "narrow")),
            P(("wide", "narrow")),
            P(("wide", "narrow"), None),
            P(),
            P(),
        ),
        out_specs=(
            P(None, "dp", ("wide", "narrow")),
            P(None, "dp", ("wide", "narrow")),
            P(None, "dp", ("wide", "narrow")),
            P(None, "wide", "narrow"),
            P(None, ("narrow", "wide")),
            P("narrow", "wide"),
            P("wide", "narrow"),
            P(("narrow", "wide")),
            P("narrow", "wide"),
            P(("wide", "narrow")),
            P(None, ("wide", "narrow")),
            P(None, ("wide", "narrow")),
            P(("wide", "narrow")),
            P(("wide", "narrow"), None),
            P(),
            P(),
        ),
        check_vma=False,
    )
```

profile of v0, /device:TPU:0, one launch (start us, length us, event | category | flops | bytes accessed | tf_op | source)
XLA Modules:
  0.0 1101.8 jit_solution(11456983785825005663)
XLA Ops:
  10.2 23.3 %all-reduce.2 = (f32[4,256]{1,0:T(4,128)S(1)}, f32[4,256]{1,0:T(4,128)S(1)}) all-reduce(f32[4,256]{1,0:T(4,128)S(1)} %get-tuple-element.142, f32[4,256]{1,0:T(4,128)S(1)} %get-tuple-element.141), channel_id=1, replica_groups=mesh['dp'=4,'wide'=4,'narrow'=2] {'wide','narrow'}, use_global_device_ids=true, to_apply=%region_3.0 | all-reduce | flops 2048 | bytes 16384 | tf_op jit(solution)/shard_map/psum | solution.py:17
  35.8 18.7 %all-gather.6.cloned.1.call-done = bf16[4,256,512]{2,1,0:T(8,128)(2,1)} async-done(((bf16[4,256,256]{2,1,0:T(8,128)(2,1)}), bf16[4,256,512]{2,1,0:T(8,128)(2,1)}) %all-gather.6.cloned.1.call-update) | async-done | bytes 1048592 | tf_op jit(solution)/shard_map/all_gather | solution.py:149
  54.4 5.6 convolution_bitcast_fusion
  64.6 72.4 %reduce-scatter.9.cloned.1.call-done = f32[1,256,1024]{2,1,0:T(8,128)} async-done(((f32[1,256,4096]{2,1,0:T(8,128)}), f32[1,256,1024]{2,1,0:T(8,128)}) %reduce-scatter.9.cloned.1.call-update) | async-done | bytes 1048592 | tf_op jit(solution)/shard_map/reduce_scatter | solution.py:154
  141.1 59.6 %reduce-scatter.7.cloned.1.call-done = f32[3,256,256]{2,1,0:T(8,128)} async-done(((f32[3,256,1024]{2,1,0:T(8,128)}), f32[3,256,256]{2,1,0:T(8,128)}) %reduce-scatter.7.cloned.1.call-update) | async-done | bytes 786448 | tf_op jit(solution)/shard_map/reduce_scatter | solution.py:153
  214.0 22.1 %all_gather.19 = bf16[256,1024]{0,1:T(8,128)(2,1)} all-gather(bf16[256,256]{0,1:T(8,128)(2,1)S(1)} %bitcast.112), channel_id=1, replica_groups=mesh['dp'=4,'wide'=4,'narrow'=2] {'wide'}, dimensions={1}, use_global_device_ids=true | all-gather | bytes 655360 | tf_op jit(solution)/shard_map/all_gather | solution.py:172
  236.2 20.9 %all-gather.8.cloned.1.call-done = bf16[256,4096]{1,0:T(8,128)(2,1)} async-done(((bf16[256,1024]{1,0:T(8,128)(2,1)}), bf16[256,4096]{1,0:T(8,128)(2,1)}) %all-gather.8.cloned.1.call-update) | async-done | bytes 2097168 | tf_op jit(solution)/shard_map/all_gather | solution.py:173
  257.1 4.2 fusion.66
  269.6 6.5 reduce-scatter.11.cloned.1.call-done
  288.1 68.3 %all-reduce.9.cloned.1.call-done = (f32[256,52]{0,1:T(8,128)}, f32[256]{0:T(256)}, f32[256,52]{0,1:T(8,128)}) async-done(((f32[256,52]{0,1:T(8,128)}, f32[256]{0:T(256)}, f32[256,52]{0,1:T(8,128)}), (f32[256,52]{0,1:T(8,128)}, f32[256]{0:T(256)}, f32[256,52]{0,1:T(8,128)})) %all-reduce.9.cloned.1.call-update) | async-done | bytes 107536 | tf_op jit(solution)/shard_map/psum | solution.py:17
  370.7 5.6 all_gather.21
  377.9 5.5 fusion.69
  383.4 21.7 %reduce-scatter.13.cloned.1.call-done = f32[256,256]{1,0:T(8,128)} async-done(((f32[256,1024]{1,0:T(8,128)}), f32[256,256]{1,0:T(8,128)}) %reduce-scatter.13.cloned.1.call-update) | async-done | bytes 262160 | tf_op jit(solution)/shard_map/reduce_scatter | solution.py:227
  425.3 58.1 %reduce-scatter.15.cloned.1.call-done = f32[256,1024]{1,0:T(8,128)} async-done(((f32[256,4096]{1,0:T(8,128)}), f32[256,1024]{1,0:T(8,128)}) %reduce-scatter.15.cloned.1.call-update) | async-done | bytes 1048592 | tf_op jit(solution)/shard_map/reduce_scatter | solution.py:230
  487.0 36.9 %all-gather.10.cloned.1.call-done = bf16[3,256,1024]{2,1,0:T(8,128)(2,1)} async-done(((bf16[3,256,256]{2,1,0:T(8,128)(2,1)}), bf16[3,256,1024]{2,1,0:T(8,128)(2,1)}) %all-gather.10.cloned.1.call-update) | async-done | bytes 1572880 | tf_op jit(solution)/shard_map/all_gather | solution.py:249
  527.5 42.7 %all-gather.12.cloned.1.call-done = bf16[256,4096]{1,0:T(8,128)(2,1)} async-done(((bf16[256,1024]{1,0:T(8,128)(2,1)}), bf16[256,4096]{1,0:T(8,128)(2,1)}) %all-gather.12.cloned.1.call-update) | async-done | bytes 2097168 | tf_op jit(solution)/shard_map/all_gather | solution.py:250
  570.2 4.1 convolution_bitcast_fusion.1
  580.9 4.7 fusion.71
  589.4 17.2 %reduce-scatter.17.cloned.1.call-done = f32[4,256,256]{2,1,0:T(8,128)} async-done(((f32[4,256,512]{2,1,0:T(8,128)}), f32[4,256,256]{2,1,0:T(8,128)}) %reduce-scatter.17.cloned.1.call-update) | async-done | bytes 1048592 | tf_op jit(solution)/shard_map/reduce_scatter | solution.py:263
  609.3 5.6 fusion.31
  626.4 20.7 %all-reduce = (f32[4,256]{1,0:T(4,128)S(1)}, f32[4,256]{1,0:T(4,128)S(1)}) all-reduce(f32[4,256]{1,0:T(4,128)S(1)} %get-tuple-element.138, f32[4,256]{1,0:T(4,128)S(1)} %get-tuple-element.139), channel_id=1, replica_groups=mesh['dp'=4,'wide'=4,'narrow'=2] {'wide','narrow'}, use_global_device_ids=true, to_apply=%region_21.22 | all-reduce | flops 2048 | bytes 16384 | tf_op jit(solution)/shard_map/psum | solution.py:17
  648.8 423.5 %all-reduce.13.cloned.1.call-done = (f32[3,512,1024]{2,1,0:T(8,128)}, f32[1024,512]{1,0:T(8,128)}, f32[512,4096]{1,0:T(8,128)}, f32[4096,512]{1,0:T(8,128)}) async-done(((f32[3,512,1024]{2,1,0:T(8,128)}, f32[1024,512]{1,0:T(8,128)}, f32[512,4096]{1,0:T(8,128)}, f32[4096,512]{1,0:T(8,128)}), (f32[3,512,1024]{2,1,0:T(8,128)}, f32[1024,512]{1,0:T(8,128)}, f32[512,4096]{1,0:T(8,128)}, ...) | async-done | bytes 25165840 | tf_op jit(solution)/shard_map/psum | solution.py:275
  1072.3 7.1 copy.244
  1081.3 4.3 copy.247
  (248 shorter events, 128.0 us)
Async XLA Ops:
  7.2 52.9 %copy-start = (bf16[3,512,1024]{2,1,0:T(8,128)(2,1)S(1)}, bf16[3,512,1024]{2,1,0:T(8,128)(2,1)}, u32[]{:S(2)}) copy-start(bf16[3,512,1024]{2,1,0:T(8,128)(2,1)} %param.21) | copy-start | bytes 9437188
  7.2 47.2 %all-gather.6.cloned.1.call-start = ((), (), s32[]{:S(2)}) async-start(), calls=%async_computation.6 | async-start | bytes 1572864 | tf_op jit(solution)/shard_map/all_gather | solution.py:149
  35.7 101.2 %reduce-scatter.9.cloned.1.call-start = ((), (), s32[]{:S(2)}) async-start(), calls=%async_computation.8 | async-start | bytes 5242880 | tf_op jit(solution)/shard_map/reduce_scatter | solution.py:154
  60.0 140.7 %reduce-scatter.7.cloned.1.call-start = ((), (), s32[]{:S(2)}) async-start(), calls=%async_computation.7 | async-start | bytes 3932160 | tf_op jit(solution)/shard_map/reduce_scatter | solution.py:153
  63.9 75.4 %copy-start.52 = (bf16[3,256]{1,0:T(4,128)(2,1)S(1)}, bf16[3,256]{1,0:T(4,128)(2,1)}, u32[]{:S(2)}) copy-start(bf16[3,256]{1,0:T(4,128)(2,1)} %param.22) | copy-start | bytes 4612
  63.9 193.2 %all-gather.8.cloned.1.call-start = ((), (), s32[]{:S(2)}) async-start(), calls=%async_computation.9 | async-start | bytes 2621440 | tf_op jit(solution)/shard_map/all_gather | solution.py:173
  64.6 138.0 %copy-start.41 = (f32[1024]{0:T(1024)}, f32[1024]{0:T(1024)S(1)}, u32[]{:S(2)}) copy-start(f32[1024]{0:T(1024)S(1)} %convert_element_type.100) | copy-start | bytes 12292
  139.2 136.9 %reduce-scatter.11.cloned.1.call-start = ((), (), s32[]{:S(2)}) async-start(), calls=%async_computation.10 | async-start | bytes 786432 | tf_op jit(solution)/shard_map/reduce_scatter | solution.py:179
  262.6 93.8 %all-reduce.9.cloned.1.call-start = ((), (), s32[]{:S(2)}) async-start(), calls=%async_computation.16 | async-start | bytes 231424 | tf_op jit(solution)/shard_map/psum | solution.py:17
  277.9 90.4 %copy-start.9 = (f32[256,256]{1,0:T(8,128)}, f32[256,256]{1,0:T(8,128)S(1)}, u32[]{:S(2)}) copy-start(f32[256,256]{1,0:T(8,128)S(1)} %get-tuple-element.171) | copy-start | bytes 786436
  286.7 118.5 %reduce-scatter.13.cloned.1.call-start = ((), (), s32[]{:S(2)}) async-start(), calls=%async_computation.11 | async-start | bytes 1310720 | tf_op jit(solution)/shard_map/reduce_scatter | solution.py:227
  365.9 10.5 copy-start.12
  377.8 105.6 %reduce-scatter.15.cloned.1.call-start = ((), (), s32[]{:S(2)}) async-start(), calls=%async_computation.13 | async-start | bytes 5242880 | tf_op jit(solution)/shard_map/reduce_scatter | solution.py:230
  383.4 140.5 %all-gather.10.cloned.1.call-start = ((), (), s32[]{:S(2)}) async-start(), calls=%async_computation.12 | async-start | bytes 1966080 | tf_op jit(solution)/shard_map/all_gather | solution.py:249
  425.3 144.9 %all-gather.12.cloned.1.call-start = ((), (), s32[]{:S(2)}) async-start(), calls=%async_computation.15 | async-start | bytes 2621440 | tf_op jit(solution)/shard_map/all_gather | solution.py:250
  486.9 119.6 %reduce-scatter.17.cloned.1.call-start = ((), (), s32[]{:S(2)}) async-start(), calls=%async_computation.14 | async-start | bytes 3145728 | tf_op jit(solution)/shard_map/reduce_scatter | solution.py:263
  527.5 46.8 %copy-start.5 = (f32[3,256,512]{2,1,0:T(8,128)S(1)}, f32[3,256,512]{2,1,0:T(8,128)}, u32[]{:S(2)}) copy-start(f32[3,256,512]{2,1,0:T(8,128)} %fusion.68) | copy-start | bytes 4718596
  575.9 72.9 %all-reduce.11.cloned.1.call-start = ((), (), s32[]{:S(2)}) async-start(), calls=%async_computation.17 | async-start | bytes 209920 | tf_op jit(solution)/shard_map/psum | solution.py:275
  585.6 21.0 %copy-start.3 = (bf16[4,256,256]{2,1,0:T(8,128)(2,1)S(1)}, bf16[4,256,256]{2,1,0:T(8,128)(2,1)}, u32[]{:S(2)}) copy-start(bf16[4,256,256]{2,1,0:T(8,128)(2,1)} %param.18) | copy-start | bytes 1572868
  585.6 23.7 %copy-start.15 = (bf16[256,4096]{1,0:T(8,128)(2,1)S(1)}, bf16[256,4096]{1,0:T(8,128)(2,1)}, u32[]{:S(2)}) copy-start(bf16[256,4096]{1,0:T(8,128)(2,1)} %all-gather.12.cloned.1.call-done) | copy-start | bytes 6291460
  609.2 463.0 %all-reduce.13.cloned.1.call-start = ((), (), s32[]{:S(2)}) async-start(), calls=%async_computation.18 | async-start | bytes 50331648 | tf_op jit(solution)/shard_map/psum | solution.py:275
  621.9 25.3 %copy-start.8 = (f32[4,256,256]{2,1,0:T(8,128)S(1)}, f32[4,256,256]{2,1,0:T(8,128)}, u32[]{:S(2)}) copy-start(f32[4,256,256]{2,1,0:T(8,128)} %reduce-scatter.17.cloned.1.call-done) | copy-start | bytes 3145732
  625.5 22.3 %copy-start.30 = (f32[256,256]{1,0:T(8,128)S(1)}, f32[256,256]{1,0:T(8,128)}, u32[]{:S(2)}) copy-start(f32[256,256]{1,0:T(8,128)} %get-tuple-element.165) | copy-start | bytes 786436
  1072.3 9.0 copy-start.4
  (49 other events, 169.3 us)
Sparse Core Ops, SparseCore 0:
  35.8 18.5 all-gather.5
  60.1 76.7 reduce-scatter.8
  139.9 60.7 reduce-scatter.6
  202.8 54.2 all-gather.7
  262.7 13.3 reduce-scatter.10
  286.8 69.5 all-reduce.8
  377.9 27.1 reduce-scatter.12
  408.0 75.4 reduce-scatter.14
  485.7 38.1 all-gather.9
  526.0 44.1 all-gather.11
  576.0 30.5 reduce-scatter.16
  610.6 30.8 all-reduce.10
  645.6 426.6 all-reduce.12
where the time goes:
time: 1100 us
  waiting for transfers between devices  847 us (77%)
  matrix products  75 us (7%)
  blocking collectives  71.8 us (7%)
  local copies, waits for them, and re-layouts  54.5 us (5%)
  other arithmetic  38.3 us (3%)
  between operations  14.6 us (1%)
    psum x2, waiting for transfers between devices, per_device(): lax.psum((qkv_weight_grad, qkv_bias_grad, out_weight_grad, up_weight_grad...  423 us
    reduce_scatter x1, waiting for transfers between devices, per_device(): lax.psum_scatter(up_part[None], 'wide', scatter_dimension=2, tiled=True)  72.4 us
    psum x1, waiting for transfers between devices, model_sum(): return lax.psum(parts, ('wide', 'narrow'))  68.3 us
    reduce_scatter x1, waiting for transfers between devices, per_device(): lax.psum_scatter(qkv_part, 'wide', scatter_dimension=2, tiled=True)  59.6 us
    reduce_scatter x1, waiting for transfers between devices, per_device(): lax.psum_scatter(contract_cols(branch_near, w_down), 'wide', scatter_dime...  58.1 us
    psum x2, blocking collectives, model_sum(): return lax.psum(parts, ('wide', 'narrow'))  44 us
    all_gather x1, waiting for transfers between devices, per_device(): lax.all_gather(up_grad[None], 'wide', axis=2, tiled=True)  42.7 us
    all_gather x1, waiting for transfers between devices, per_device(): lax.all_gather(projected_grad, 'wide', axis=2, tiled=True)  36.9 us
  transfers between devices with their start and end apart: 13, of which 12 were waited for; matrix products, arithmetic and copies ran while one was open for 8% of the time, Pallas kernels for 0%

commit v1 on v0

--- a/solution.py
+++ b/solution.py
@@ -3,6 +3,7 @@
 import jax.numpy as jnp
 from jax import lax
 from jax.sharding import PartitionSpec as P
+from jax.lax import axis_index, axis_size, ppermute
 
 D = 2048
 HD = 128
@@ -245,8 +246,35 @@
         jnp.bfloat16
     )
     qkv_bias_grad = jnp.sum(projected_grad.astype(jnp.float32), axis=1)
+
+    def define_the_run(arr_in, axis_key):
+        front = axis_size(axis_key)
+        carry_in = axis_index(axis_key)
+        vec_out, everything, state_now = (front, carry_in, arr_in.shape[2])
+        xs_all = [(w, (w + 1) % vec_out) for w in range(vec_out)]
+        parts_seen = [(w, (w - 1) % vec_out) for w in range(vec_out)]
+        all_values = jnp.zeros(
+            (*arr_in.shape[:2], vec_out * state_now, *arr_in.shape[3:]), arr_in.dtype
+        )
+        all_values = lax.dynamic_update_slice_in_dim(
+            all_values, arr_in, everything * state_now, axis=2
+        )
+        odd = piece_next = arr_in
+        current_arr = vec_out // 2
+        for m in tuple(range(1, current_arr + 1)):
+            odd = ppermute(odd, axis_key, xs_all)
+            all_values = lax.dynamic_update_slice_in_dim(
+                all_values, odd, (everything - m) % vec_out * state_now, axis=2
+            )
+            if m < vec_out - current_arr:
+                piece_next = ppermute(piece_next, axis_key, parts_seen)
+                all_values = lax.dynamic_update_slice_in_dim(
+                    all_values, piece_next, (everything + m) % vec_out * state_now, axis=2
+                )
+        return all_values
+
     far_qkv, far_up = (
-        lax.all_gather(projected_grad, "wide", axis=2, tiled=True),
+        define_the_run(projected_grad, "wide"),
         lax.all_gather(up_grad[None], "wide", axis=2, tiled=True),
     )
     qkv_weight_grad = jnp.einsum(

time: 1100 us -> 1100 us (level)
  waiting for transfers between devices: 847 us -> 813 us
  starting transfers between devices: 0.94 us -> 17.1 us
  local copies, waits for them, and re-layouts: 54.5 us -> 68.7 us
    all_gather x1, waiting for transfers between devices: 42.7 us -> 0.01 us  [per_device(): lax.all_gather(up_grad[None], 'wide', axis=2, tiled=True)]
    all_gather x1 -> x0, waiting for transfers between devices: 36.9 us -> none  [per_device(): lax.all_gather(projected_grad, 'wide', axis=2, tiled=True)]
    ppermute x0 -> x3, waiting for transfers between devices: none -> 26.2 us  [the longest x2 26.2 us: define_the_run(): odd = ppermute(odd, axis_key, xs_all)]
    ppermute x0 -> x3, starting transfers between devices: none -> 16.2 us  [the longest x2 12.4 us: define_the_run(): odd = ppermute(odd, axis_key, xs_all)]
    reduce_scatter x1, waiting for transfers between devices: 58.1 us -> 74.2 us  [per_device(): lax.psum_scatter(contract_cols(branch_near, w_down), 'wide', scatter_dime...]
    unnamed x139 -> x135, local copies, waits for them, and re-layouts: 30.6 us -> 30.6 us
  transfers between devices with their start and end apart: 13 -> 15, of which waited for: 12 -> 12; matrix products, arithmetic and copies ran while one was open for 8% -> 9% of each run, Pallas kernels for 0% -> 0%
where the time goes in v1:
time: 1100 us
  waiting for transfers between devices  813 us (74%)
  matrix products  77.1 us (7%)
  blocking collectives  71.8 us (7%)
  local copies, waits for them, and re-layouts  68.7 us (6%)
  other arithmetic  38.2 us (3%)
  starting transfers between devices  17.1 us (2%)
  between operations  14.9 us (1%)
    psum x2, waiting for transfers between devices, per_device(): lax.psum((qkv_weight_grad, qkv_bias_grad, out_weight_grad, up_weight_grad...  423 us
    reduce_scatter x1, waiting for transfers between devices, per_device(): lax.psum_scatter(contract_cols(branch_near, w_down), 'wide', scatter_dime...  74.2 us
    reduce_scatter x1, waiting for transfers between devices, per_device(): lax.psum_scatter(up_part[None], 'wide', scatter_dimension=2, tiled=True)  72.4 us
    psum x1, waiting for transfers between devices, model_sum(): return lax.psum(parts, ('wide', 'narrow'))  68.4 us
    reduce_scatter x1, waiting for transfers between devices, per_device(): lax.psum_scatter(qkv_part, 'wide', scatter_dimension=2, tiled=True)  59.6 us
    psum x2, blocking collectives, model_sum(): return lax.psum(parts, ('wide', 'narrow'))  44 us
    unnamed x135, local copies, waits for them, and re-layouts  30.6 us
    reduce_scatter x1, waiting for transfers between devices, per_device(): lax.psum_scatter(contract_cols(branch_near, w_out), 'wide', scatter_dimen...  27 us
  transfers between devices with their start and end apart: 15, of which 12 were waited for; matrix products, arithmetic and copies ran while one was open for 9% of the time, Pallas kernels for 0%

profile of v1, /device:TPU:0, one launch (start us, length us, event | category | flops | bytes accessed | tf_op | source)
XLA Modules:
  0.0 1100.4 jit_solution(6887730244269682571)
XLA Ops:
  10.2 23.3 %all-reduce.2 = (f32[4,256]{1,0:T(4,128)S(1)}, f32[4,256]{1,0:T(4,128)S(1)}) all-reduce(f32[4,256]{1,0:T(4,128)S(1)} %get-tuple-element.142, f32[4,256]{1,0:T(4,128)S(1)} %get-tuple-element.141), channel_id=1, replica_groups=mesh['dp'=4,'wide'=4,'narrow'=2] {'wide','narrow'}, use_global_device_ids=true, to_apply=%region_3.0 | all-reduce | flops 2048 | bytes 16384 | tf_op jit(solution)/shard_map/psum | solution.py:18
  35.8 18.7 %all-gather.5.cloned.1.call-done = bf16[4,256,512]{2,1,0:T(8,128)(2,1)} async-done(((bf16[4,256,256]{2,1,0:T(8,128)(2,1)}), bf16[4,256,512]{2,1,0:T(8,128)(2,1)}) %all-gather.5.cloned.1.call-update) | async-done | bytes 1048592 | tf_op jit(solution)/shard_map/all_gather | solution.py:150
  54.4 5.6 convolution_bitcast_fusion
  64.6 72.4 %reduce-scatter.9.cloned.1.call-done = f32[1,256,1024]{2,1,0:T(8,128)} async-done(((f32[1,256,4096]{2,1,0:T(8,128)}), f32[1,256,1024]{2,1,0:T(8,128)}) %reduce-scatter.9.cloned.1.call-update) | async-done | bytes 1048592 | tf_op jit(solution)/shard_map/reduce_scatter | solution.py:155
  141.1 59.6 %reduce-scatter.7.cloned.1.call-done = f32[3,256,256]{2,1,0:T(8,128)} async-done(((f32[3,256,1024]{2,1,0:T(8,128)}), f32[3,256,256]{2,1,0:T(8,128)}) %reduce-scatter.7.cloned.1.call-update) | async-done | bytes 786448 | tf_op jit(solution)/shard_map/reduce_scatter | solution.py:154
  214.0 22.1 %all_gather.16 = bf16[256,1024]{0,1:T(8,128)(2,1)} all-gather(bf16[256,256]{0,1:T(8,128)(2,1)S(1)} %bitcast.110), channel_id=1, replica_groups=mesh['dp'=4,'wide'=4,'narrow'=2] {'wide'}, dimensions={1}, use_global_device_ids=true | all-gather | bytes 655360 | tf_op jit(solution)/shard_map/all_gather | solution.py:173
  236.2 20.9 %all-gather.7.cloned.1.call-done = bf16[256,4096]{1,0:T(8,128)(2,1)} async-done(((bf16[256,1024]{1,0:T(8,128)(2,1)}), bf16[256,4096]{1,0:T(8,128)(2,1)}) %all-gather.7.cloned.1.call-update) | async-done | bytes 2097168 | tf_op jit(solution)/shard_map/all_gather | solution.py:174
  269.5 6.5 reduce-scatter.11.cloned.1.call-done
  288.1 68.4 %all-reduce.9.cloned.1.call-done = (f32[256,52]{0,1:T(8,128)}, f32[256]{0:T(256)}, f32[256,52]{0,1:T(8,128)}) async-done(((f32[256,52]{0,1:T(8,128)}, f32[256]{0:T(256)}, f32[256,52]{0,1:T(8,128)}), (f32[256,52]{0,1:T(8,128)}, f32[256]{0:T(256)}, f32[256,52]{0,1:T(8,128)})) %all-reduce.9.cloned.1.call-update) | async-done | bytes 107536 | tf_op jit(solution)/shard_map/psum | solution.py:18
  370.6 5.6 all_gather.18
  376.3 5.5 fusion.69
  384.6 74.2 %reduce-scatter.15.cloned.1.call-done = f32[256,1024]{1,0:T(8,128)} async-done(((f32[256,4096]{1,0:T(8,128)}), f32[256,1024]{1,0:T(8,128)}) %reduce-scatter.15.cloned.1.call-update) | async-done | bytes 1048592 | tf_op jit(solution)/shard_map/reduce_scatter | solution.py:231
  462.2 27.0 %reduce-scatter.13.cloned.1.call-done = f32[256,256]{1,0:T(8,128)} async-done(((f32[256,1024]{1,0:T(8,128)}), f32[256,256]{1,0:T(8,128)}) %reduce-scatter.13.cloned.1.call-update) | async-done | bytes 262160 | tf_op jit(solution)/shard_map/reduce_scatter | solution.py:228
  510.6 18.7 %collective-permute-done = bf16[3,256,256]{1,2,0:T(8,128)(2,1)} collective-permute-done((bf16[3,256,256]{1,2,0:T(8,128)(2,1)}, bf16[3,256,256]{1,2,0:T(8,128)(2,1)}, u32[]{:S(2)}, u32[]{:S(2)}) %collective-permute-start) | collective-permute-done | bytes 393248 | tf_op jit(solution)/shard_map/ppermute | solution.py:265
  529.3 12.4 %collective-permute-start.2 = (bf16[3,256,256]{1,2,0:T(8,128)(2,1)}, bf16[3,256,256]{1,2,0:T(8,128)(2,1)}, u32[]{:S(2)}, u32[]{:S(2)}) collective-permute-start(bf16[3,256,256]{1,2,0:T(8,128)(2,1)} %collective-permute-done), channel_id=1, source_target_pairs={{0,2},{2,4},{4,6},{6,0},{1,3},{3,5},{5,7},{7,1},{8,10},{10,12},{12... | collective-permute-start | bytes 1179656 | tf_op jit(solution)/shard_map/ppermute | solution.py:265
  554.1 7.5 collective-permute-done.2
  579.6 4.7 fusion.71
  584.3 5.4 fusion.73
  589.7 15.1 %reduce-scatter.17.cloned.1.call-done = f32[4,256,256]{2,1,0:T(8,128)} async-done(((f32[4,256,512]{2,1,0:T(8,128)}), f32[4,256,256]{2,1,0:T(8,128)}) %reduce-scatter.17.cloned.1.call-update) | async-done | bytes 1048592 | tf_op jit(solution)/shard_map/reduce_scatter | solution.py:291
  607.5 5.6 fusion.31
  624.6 20.7 %all-reduce = (f32[4,256]{1,0:T(4,128)S(1)}, f32[4,256]{1,0:T(4,128)S(1)}) all-reduce(f32[4,256]{1,0:T(4,128)S(1)} %get-tuple-element.138, f32[4,256]{1,0:T(4,128)S(1)} %get-tuple-element.139), channel_id=1, replica_groups=mesh['dp'=4,'wide'=4,'narrow'=2] {'wide','narrow'}, use_global_device_ids=true, to_apply=%region_21.22 | all-reduce | flops 2048 | bytes 16384 | tf_op jit(solution)/shard_map/psum | solution.py:18
  647.0 423.5 %all-reduce.13.cloned.1.call-done = (f32[3,512,1024]{2,1,0:T(8,128)}, f32[1024,512]{1,0:T(8,128)}, f32[512,4096]{1,0:T(8,128)}, f32[4096,512]{1,0:T(8,128)}) async-done(((f32[3,512,1024]{2,1,0:T(8,128)}, f32[1024,512]{1,0:T(8,128)}, f32[512,4096]{1,0:T(8,128)}, f32[4096,512]{1,0:T(8,128)}), (f32[3,512,1024]{2,1,0:T(8,128)}, f32[1024,512]{1,0:T(8,128)}, f32[512,4096]{1,0:T(8,128)}, ...) | async-done | bytes 25165840 | tf_op jit(solution)/shard_map/psum | solution.py:303
  1070.5 7.1 copy.251
  1079.5 4.3 copy.254
  (253 shorter events, 150.9 us)
Async XLA Ops:
  7.2 52.9 %copy-start = (bf16[3,512,1024]{2,1,0:T(8,128)(2,1)S(1)}, bf16[3,512,1024]{2,1,0:T(8,128)(2,1)}, u32[]{:S(2)}) copy-start(bf16[3,512,1024]{2,1,0:T(8,128)(2,1)} %param.21) | copy-start | bytes 9437188
  7.2 47.2 %all-gather.5.cloned.1.call-start = ((), (), s32[]{:S(2)}) async-start(), calls=%async_computation.6 | async-start | bytes 1572864 | tf_op jit(solution)/shard_map/all_gather | solution.py:150
  35.7 101.2 %reduce-scatter.9.cloned.1.call-start = ((), (), s32[]{:S(2)}) async-start(), calls=%async_computation.8 | async-start | bytes 5242880 | tf_op jit(solution)/shard_map/reduce_scatter | solution.py:155
  60.0 140.7 %reduce-scatter.7.cloned.1.call-start = ((), (), s32[]{:S(2)}) async-start(), calls=%async_computation.7 | async-start | bytes 3932160 | tf_op jit(solution)/shard_map/reduce_scatter | solution.py:154
  63.9 75.4 %copy-start.50 = (bf16[3,256]{1,0:T(4,128)(2,1)S(1)}, bf16[3,256]{1,0:T(4,128)(2,1)}, u32[]{:S(2)}) copy-start(bf16[3,256]{1,0:T(4,128)(2,1)} %param.22) | copy-start | bytes 4612
  63.9 193.2 %all-gather.7.cloned.1.call-start = ((), (), s32[]{:S(2)}) async-start(), calls=%async_computation.9 | async-start | bytes 2621440 | tf_op jit(solution)/shard_map/all_gather | solution.py:174
  64.6 138.0 %copy-start.39 = (f32[1024]{0:T(1024)}, f32[1024]{0:T(1024)S(1)}, u32[]{:S(2)}) copy-start(f32[1024]{0:T(1024)S(1)} %convert_element_type.100) | copy-start | bytes 12292
  139.2 136.9 %reduce-scatter.11.cloned.1.call-start = ((), (), s32[]{:S(2)}) async-start(), calls=%async_computation.10 | async-start | bytes 786432 | tf_op jit(solution)/shard_map/reduce_scatter | solution.py:180
  262.6 93.8 %all-reduce.9.cloned.1.call-start = ((), (), s32[]{:S(2)}) async-start(), calls=%async_computation.15 | async-start | bytes 231424 | tf_op jit(solution)/shard_map/psum | solution.py:18
  277.9 90.3 %copy-start.9 = (f32[256,256]{1,0:T(8,128)}, f32[256,256]{1,0:T(8,128)S(1)}, u32[]{:S(2)}) copy-start(f32[256,256]{1,0:T(8,128)S(1)} %get-tuple-element.171) | copy-start | bytes 786436
  286.7 172.1 %reduce-scatter.15.cloned.1.call-start = ((), (), s32[]{:S(2)}) async-start(), calls=%async_computation.12 | async-start | bytes 5242880 | tf_op jit(solution)/shard_map/reduce_scatter | solution.py:231
  381.8 107.5 %reduce-scatter.13.cloned.1.call-start = ((), (), s32[]{:S(2)}) async-start(), calls=%async_computation.11 | async-start | bytes 1310720 | tf_op jit(solution)/shard_map/reduce_scatter | solution.py:228
  384.5 184.3 %all-gather.9.cloned.1.call-start = ((), (), s32[]{:S(2)}) async-start(), calls=%async_computation.14 | async-start | bytes 2621440 | tf_op jit(solution)/shard_map/all_gather | solution.py:278
  462.2 142.6 %reduce-scatter.17.cloned.1.call-start = ((), (), s32[]{:S(2)}) async-start(), calls=%async_computation.13 | async-start | bytes 3145728 | tf_op jit(solution)/shard_map/reduce_scatter | solution.py:291
  506.8 22.5 %collective-permute-start = (bf16[3,256,256]{1,2,0:T(8,128)(2,1)}, bf16[3,256,256]{1,2,0:T(8,128)(2,1)}, u32[]{:S(2)}, u32[]{:S(2)}) collective-permute-start(bf16[3,256,256]{1,2,0:T(8,128)(2,1)} %get-tuple-element.169), channel_id=1, source_target_pairs={{0,2},{2,4},{4,6},{6,0},{1,3},{3,5},{5,7},{7,1},{8,10},{10,12},{12... | collective-permute-start | bytes 1179656 | tf_op jit(solution)/shard_map/ppermute | solution.py:265
  506.8 41.8 %collective-permute-start.1 = (bf16[3,256,256]{1,2,0:T(8,128)(2,1)}, bf16[3,256,256]{1,2,0:T(8,128)(2,1)}, u32[]{:S(2)}, u32[]{:S(2)}) collective-permute-start(bf16[3,256,256]{1,2,0:T(8,128)(2,1)} %get-tuple-element.169), channel_id=1, source_target_pairs={{0,6},{2,0},{4,2},{6,4},{1,7},{3,1},{5,3},{7,5},{8,14},{10,8},{12,... | collective-permute-start | bytes 1179656 | tf_op jit(solution)/shard_map/ppermute | solution.py:270
  529.3 32.3 %collective-permute-start.2 = (bf16[3,256,256]{1,2,0:T(8,128)(2,1)}, bf16[3,256,256]{1,2,0:T(8,128)(2,1)}, u32[]{:S(2)}, u32[]{:S(2)}) collective-permute-start(bf16[3,256,256]{1,2,0:T(8,128)(2,1)} %collective-permute-done), channel_id=1, source_target_pairs={{0,2},{2,4},{4,6},{6,0},{1,3},{3,5},{5,7},{7,1},{8,10},{10,12},{12... | collective-permute-start | bytes 1179656 | tf_op jit(solution)/shard_map/ppermute | solution.py:265
  574.7 72.4 %all-reduce.11.cloned.1.call-start = ((), (), s32[]{:S(2)}) async-start(), calls=%async_computation.16 | async-start | bytes 209920 | tf_op jit(solution)/shard_map/psum | solution.py:303
  584.3 20.4 %copy-start.3 = (bf16[4,256,256]{2,1,0:T(8,128)(2,1)S(1)}, bf16[4,256,256]{2,1,0:T(8,128)(2,1)}, u32[]{:S(2)}) copy-start(bf16[4,256,256]{2,1,0:T(8,128)(2,1)} %param.18) | copy-start | bytes 1572868
  584.3 23.2 %copy-start.14 = (bf16[256,4096]{1,0:T(8,128)(2,1)S(1)}, bf16[256,4096]{1,0:T(8,128)(2,1)}, u32[]{:S(2)}) copy-start(bf16[256,4096]{1,0:T(8,128)(2,1)} %all-gather.9.cloned.1.call-done) | copy-start | bytes 6291460
  607.4 463.1 %all-reduce.13.cloned.1.call-start = ((), (), s32[]{:S(2)}) async-start(), calls=%async_computation.17 | async-start | bytes 50331648 | tf_op jit(solution)/shard_map/psum | solution.py:303
  620.1 25.3 %copy-start.8 = (f32[4,256,256]{2,1,0:T(8,128)S(1)}, f32[4,256,256]{2,1,0:T(8,128)}, u32[]{:S(2)}) copy-start(f32[4,256,256]{2,1,0:T(8,128)} %reduce-scatter.17.cloned.1.call-done) | copy-start | bytes 3145732
  623.8 22.3 %copy-start.28 = (f32[256,256]{1,0:T(8,128)S(1)}, f32[256,256]{1,0:T(8,128)}, u32[]{:S(2)}) copy-start(f32[256,256]{1,0:T(8,128)} %get-tuple-element.165) | copy-start | bytes 786436
  1070.5 9.0 copy-start.4
  (49 other events, 168.9 us)
Sparse Core Ops, SparseCore 0:
  35.8 18.5 all-gather.4
  60.1 76.7 reduce-scatter.8
  139.9 60.7 reduce-scatter.6
  202.8 54.2 all-gather.6
  262.7 13.3 reduce-scatter.10
  286.8 69.6 all-reduce.8
  381.9 76.7 reduce-scatter.14
  461.6 27.6 reduce-scatter.12
  491.5 67.5 all-gather.8
  574.8 29.9 reduce-scatter.16
  608.9 30.8 all-reduce.10
  643.8 426.6 all-reduce.12
